TPU v7x, 512 devices: a whole 4x4x16 slice. The times are simulated.
512 devices in a mesh: gx: 4 (over z_hi, core), gy: 16 (over x, y), gz: 8 (over z_lo).
Axes of the slice: x: 4, y: 4, z: 16 (z_hi: 2, z_lo: 8; z = z_hi * 8 + z_lo), core: 2. Of those that a mesh axis runs over, the one named last changes fastest.
Arguments:
- positions: float32 [4, 16, 8, 3, 128], P('gx', 'gy', 'gz'), as said below
- species: int32 [4, 16, 8, 128], P('gx', 'gy', 'gz'), may hold values from 0 to 5
- counts: int32 [4, 16, 8], P('gx', 'gy', 'gz'), may hold values from 64 to 128, as said below
- neighbours: int32 [4, 16, 8, 18, 128], P('gx', 'gy', 'gz'), may hold values from 0 to 1151, as said below
- send_lists: int32 [4, 16, 8, 2, 2, 2, 16], P('gx', 'gy', 'gz'), may hold values from 0 to 127, as said below
- embed: bfloat16 [6, 128], replicated, may hold values from -4 to 4
- radial_in: bfloat16 [2, 8, 64], replicated, may hold values from -6 to 6
- radial_mid: bfloat16 [2, 64, 64], replicated, may hold values from -0.75 to 0.75
- radial_out: bfloat16 [2, 64, 512], replicated, may hold values from -0.75 to 0.75
- up_w: bfloat16 [2, 2, 128, 128], replicated, may hold values from -0.5 to 0.5
- mix_w: bfloat16 [2, 2, 128, 128], replicated, may hold values from -0.5 to 0.5
- out_w: bfloat16 [2, 2, 128, 128], replicated, may hold values from -0.5 to 0.5
- skip_w: bfloat16 [2, 2, 128, 128], replicated, may hold values from -0.5 to 0.5
- product_w: float32 [2, 3, 128], replicated, may hold values from -0.5 to 0.5
- read_one: float32 [128], replicated, may hold values from -0.5 to 0.5
- read_hidden: bfloat16 [128, 16], replicated, may hold values from -0.5 to 0.5
- read_out: float32 [16], replicated, may hold values from -1.5 to 1.5
Outputs:
- energies: float32 [4, 16, 8, 128], P('gx', 'gy', 'gz')
- forces: float32 [4, 16, 8, 3, 128], P('gx', 'gy', 'gz')
- pass_gradient: float32 [4, 16, 8, 4, 128, 128], P('gx', 'gy', 'gz')
Inputs may be any that keep to these rules, and one draw needn't show every extreme that they name: `positions`: atom slot a of a brick sits near a lattice site of spacing 3.0 (a different site for each slot), each coordinate within 0.45 of it. `counts`: slots below the count are occupied; some brick has all 128 slots occupied. `neighbours`: each atom lists the 18 sites within 1.5 lattice spacings, occupied or not, as a local slot or as A plus the ghost slot that holds it. `send_lists`: the eight cells together list every slot of the brick exactly once.
All inputs are finite; a program needn't handle non-finite values.
Results may differ from a plain program's by a relative error of at most 0.024.
Values may be sent and summed in bfloat16 or wider, within the bound.
No kernel may reach another device: no remote copies, remote signals or barrier semaphores. Data moves between devices by JAX's collectives and lax.ppermute only.
A program may use at most 128 MiB of HBM per device.

v0:
```python
import math

import jax
import jax.numpy as jnp
from jax import lax
from jax.experimental import pallas as pl
from jax.experimental.pallas import tpu as pltpu
from jax.sharding import PartitionSpec as P

NRAD = 8
NBR = 18
A = 128
LX = 8
LY = 4
LZ = 4
RC = 5.0
SPACING = 3.0
C = 128
H = 64

WIDE = 12 * 12 * 16
PLANE = 12 * 16
ROWS1 = 10 * PLANE
TILE = 128
ROWS2 = 8 * TILE
ROWS3 = 6 * TILE
OWN = 4 * 4 * 16
PADR = 32
OFFSETS = [
    (dy, dz, dx)
    for dy in (-1, 0, 1)
    for dz in (-1, 0, 1)
    for dx in (-1, 0, 1)
    if 0 < dy * dy + dz * dz + dx * dx <= 2
]
BF = jnp.bfloat16
F32 = jnp.float32
SCALE = 1.0 / math.sqrt(NBR)
NORM = math.sqrt(2.0 / RC)


def mm(a, b):
    return jnp.dot(a.astype(BF), b.astype(BF), preferred_element_type=F32)


def mm_t(a, b):
    return lax.dot_general(
        a.astype(BF), b.astype(BF), (((1,), (1,)), ((), ())), preferred_element_type=F32
    )


def tmm(a, b):
    return lax.dot_general(
        a.astype(BF), b.astype(BF), (((0,), (0,)), ((), ())), preferred_element_type=F32
    )


def silu(z):
    return 0.5 * z * (1.0 + jnp.tanh(0.5 * z))


def silu_slope(z):
    gate = 0.5 + 0.5 * jnp.tanh(0.5 * z)
    return gate + z * gate * (1.0 - gate)


def sine(turns):
    near = jnp.floor(turns + 0.5)
    part = turns - near
    half = near * 0.5
    odd = (half - jnp.floor(half)) * 2.0
    w = part * math.pi
    q = w * w
    series = 1.0 + q * (
        -1.0 / 6 + q * (1.0 / 120 + q * (-1.0 / 5040 + q * (1.0 / 362880 - q / 39916800)))
    )
    return w * series * (1.0 - 2.0 * odd)


def shape_of(geo):
    d = [geo[k : k + 1] for k in range(3)]
    live = geo[3:4]
    square = d[0] * d[0] + d[1] * d[1] + d[2] * d[2]
    dist = jnp.sqrt(square)
    inv = 1.0 / dist
    u = [x * inv for x in d]
    t = jnp.minimum(dist / RC, 1.0)
    t2 = t * t
    t6 = t2 * t2 * t2
    env = 1.0 - 28.0 * t6 + 48.0 * t6 * t - 21.0 * t6 * t2
    return dist, inv, u, t, env * live, live


def orders(width):
    return (lax.broadcasted_iota(jnp.int32, (NRAD, width), 0) + 1).astype(F32)


def radial_forward(dist, inv, w_in, w_mid):
    k = orders(dist.shape[1])
    bessel = NORM * sine(k * (dist / RC)) * inv
    padded = jnp.concatenate([bessel, jnp.zeros_like(bessel)], 0)
    z1 = mm(w_in, padded)
    z2 = mm(w_mid, silu(z1))
    return bessel, z1, z2


def hidden_stack(h, env, u):
    scaled = h * env
    return jnp.concatenate(
        [scaled.astype(BF)] + [(scaled * u[k]).astype(BF) for k in range(3)], 0
    )


def radial_backward(dist, inv, u, t, env, live, bessel, z1, z2, g, w_mid_fwd, w_in_fwd):
    h = silu(z2)
    parts = [g[k * H : (k + 1) * H] for k in range(4)]
    q = [jnp.sum(h * parts[k], 0, keepdims=True) for k in range(4)]
    gh = env * (parts[0] + u[0] * parts[1] + u[1] * parts[2] + u[2] * parts[3])
    g_env = live * (q[0] + u[0] * q[1] + u[1] * q[2] + u[2] * q[3])
    g_u = [env * q[k + 1] for k in range(3)]
    gz2 = gh * silu_slope(z2)
    gz1 = mm(w_mid_fwd, gz2) * silu_slope(z1)
    gb = mm(w_in_fwd, gz1)[:NRAD]
    k = orders(dist.shape[1])
    slope = (NORM * (k * (math.pi / RC)) * sine(k * (dist / RC) + 0.5) - bessel) * inv
    rest = 1.0 - t
    t2 = t * t
    g_dist = jnp.sum(gb * slope, 0, keepdims=True) + g_env * (
        (-168.0 / RC) * t2 * t2 * t * rest * rest
    )
    along = u[0] * g_u[0] + u[1] * g_u[1] + u[2] * g_u[2]
    return [u[k] * g_dist + (g_u[k] - u[k] * along) * inv for k in range(3)]


def split_mm(perm, x):
    high = x.astype(BF)
    low = (x - high.astype(F32)).astype(BF)
    return jnp.dot(perm, high, preferred_element_type=F32) + jnp.dot(
        perm, low, preferred_element_type=F32
    )


def kernel(
    wide_ref,
    near_ref,
    own_ref,
    perm_ref,
    embed_ref,
    w_in_t_ref,
    w_mid_t_ref,
    w_in_ref,
    w_mid_ref,
    w_out_ref,
    up_ref,
    mix_ref,
    out_ref,
    skip_ref,
    prod_ref,
    read_one_ref,
    read_hidden_ref,
    read_out_ref,
    energy_ref,
    force_ref,
    gpass_ref,
    geo,
    hid,
    send,
    base,
    alv,
    feat,
    pas,
    mixed,
    dm2,
    dfeat,
    dm1,
    gp,
    en,
    wc1,
    wc2,
    geo_own,
    gh1,
    gh2,
    facc,
):
    wc1[...] = jnp.zeros((4 * H, 4 * C), BF)
    wc2[...] = jnp.zeros((4 * H, 8 * C), BF)
    wc1[0:H, 0:C] = w_out_ref[0, :, 0:C]
    wc2[0:H, 0:C] = w_out_ref[1, :, 0:C]
    wc2[0:H, 7 * C : 8 * C] = w_out_ref[1, :, 3 * C : 4 * C]
    for k in range(3):
        rows = slice((k + 1) * H, (k + 2) * H)
        wc1[rows, (k + 1) * C : (k + 2) * C] = w_out_ref[0, :, 2 * C : 3 * C]
        wc2[rows, (k + 1) * C : (k + 2) * C] = w_out_ref[1, :, C : 2 * C]
        wc2[rows, (k + 4) * C : (k + 5) * C] = w_out_ref[1, :, 2 * C : 3 * C]

    wide = wide_ref[...]
    level = lax.broadcasted_iota(jnp.int32, (16, WIDE), 0).astype(F32) + 1.0
    one_hot = (wide[3:4] == level).astype(F32).astype(BF)
    first = tmm(one_hot, embed_ref[...])
    base[...] = first
    alv[...] = tmm(one_hot, jnp.ones((16, C), BF))
    send[0:PADR] = jnp.zeros((PADR, C), F32)
    send[PADR + WIDE : PADR + WIDE + PADR] = jnp.zeros((PADR, C), F32)
    send[PADR : PADR + WIDE] = mm(first, up_ref[0, 0])

    row = lax.broadcasted_iota(jnp.int32, (8, 1), 0)

    def geometry(centre, other):
        alive = (centre > 0.5).astype(F32) * (other > 0.5).astype(F32)
        return jnp.where(row == 3, alive, other - centre)

    def stack_hidden(layer, width):
        w_in = w_in_t_ref[layer]
        w_mid = w_mid_t_ref[layer]

        def one(o, carry):
            dist, inv, u, t, env, live = shape_of(geo[o, :, :width])
            bessel, z1, z2 = radial_forward(dist, inv, w_in, w_mid)
            hid[o, :, :width] = hidden_stack(silu(z2), env, u)
            return carry

        lax.fori_loop(0, NBR, one, 0)

    centre = pltpu.roll(wide, WIDE - PLANE, 1)[:, :ROWS1]
    for o, (dy, dz, dx) in enumerate(OFFSETS):
        shift = PLANE + (dy * 12 + dz) * 16 + dx
        geo[o] = geometry(centre, pltpu.roll(wide, (-shift) % WIDE, 1)[:, :ROWS1])
    stack_hidden(0, ROWS1)

    def rows_one(tile, carry):
        start = pl.multiple_of(tile * TILE, TILE)
        m = [jnp.zeros((TILE, C), F32) for _ in range(4)]
        for o, (dy, dz, dx) in enumerate(OFFSETS):
            w = tmm(hid[o, :, pl.ds(start, TILE)], wc1[...])
            s = send[pl.ds(start + (PADR + PLANE + (dy * 12 + dz) * 16 + dx), TILE), :]
            for c in range(4):
                m[c] = m[c] + w[:, c * C : (c + 1) * C] * s
        prod = prod_ref[0]
        p0, p1, p2 = prod[0:1], prod[1:2], prod[2:3]
        a = [mm(m[c] * SCALE, mix_ref[0, min(c, 1)]) for c in range(4)]
        b_s = a[0] + p0 * a[0] * a[0] + p1 * (a[1] * a[1] + a[2] * a[2] + a[3] * a[3])
        b = [b_s] + [a[c] + p2 * a[0] * a[c] for c in range(1, 4)]
        here = pl.ds(start, TILE)
        for c in range(4):
            new = mm(b[c], out_ref[0, min(c, 1)])
            if c == 0:
                new = new + mm(base[pl.ds(start + PLANE, TILE), :], skip_ref[0, 0])
                feat[here, :] = new
            mixed[c, here, :] = a[c]
            pas[c, here, :] = mm(new, up_ref[1, min(c, 1)]).astype(BF).astype(F32)
        return carry

    lax.fori_loop(0, ROWS1 // TILE, rows_one, 0)

    centre = near_ref[1, :, 2 * TILE : 2 * TILE + ROWS2]
    for o, (dy, dz, dx) in enumerate(OFFSETS):
        shift = 2 * TILE + dy * TILE + dx
        other = pltpu.roll(near_ref[dz + 1], (-shift) % (12 * TILE), 1)[:, :ROWS2]
        geo[o, :, :ROWS2] = geometry(centre, other)
    stack_hidden(1, ROWS2)
    for c in range(4):
        dm2[c, 0:PADR] = jnp.zeros((PADR, C), F32)
        dm2[c, PADR + ROWS2 :] = jnp.zeros((PADR, C), F32)
        dm1[c, 0:PADR] = jnp.zeros((PADR, C), F32)
        dm1[c, PADR + ROWS3 :] = jnp.zeros((PADR, C), F32)

    def rows_two(plane, carry):
        start = pl.multiple_of(plane * TILE, TILE)
        at = pl.multiple_of((plane + 1) * PLANE + 32, 32)
        m = [jnp.zeros((TILE, C), F32) for _ in range(4)]
        for o, (dy, dz, dx) in enumerate(OFFSETS):
            w = tmm(hid[o, :, pl.ds(start, TILE)], wc2[...])
            w = [w[:, c * C : (c + 1) * C] for c in range(8)]
            there = pl.ds(at + ((dy * 12 + dz) * 16 + dx), TILE)
            p = [pas[c, there, :] for c in range(4)]
            m[0] = m[0] + w[0] * p[0] + w[1] * p[1] + w[2] * p[2] + w[3] * p[3]
            for k in range(1, 4):
                m[k] = m[k] + w[k + 3] * p[0] + w[7] * p[k]
        prod = prod_ref[1]
        p0, p1 = prod[0:1], prod[1:2]
        a = [mm(m[c] * SCALE, mix_ref[1, min(c, 1)]) for c in range(4)]
        b_s = a[0] + p0 * a[0] * a[0] + p1 * (a[1] * a[1] + a[2] * a[2] + a[3] * a[3])
        s1 = feat[pl.ds(at, TILE), :]
        s2 = mm(b_s, out_ref[1, 0]) + mm(s1, skip_ref[1, 0])
        zh = mm(s2, read_hidden_ref[...])
        alive = alv[pl.ds(at + PLANE, TILE), :]
        site = jnp.sum(s1 * read_one_ref[...] + silu(zh) * read_out_ref[...], 1, keepdims=True)
        here = pl.ds(start, TILE)
        en[here, :] = alive * site
        gs2 = mm_t(alive * read_out_ref[...] * silu_slope(zh), read_hidden_ref[...])
        gb = mm_t(gs2, out_ref[1, 0])
        dfeat[here, :] = alive * read_one_ref[...] + mm_t(gs2, skip_ref[1, 0])
        inner = pl.ds(start + PADR, TILE)
        dm2[0, inner, :] = mm_t(gb * (1.0 + 2.0 * p0 * a[0]), mix_ref[1, 0]) * SCALE
        for k in range(1, 4):
            dm2[k, inner, :] = mm_t(gb * (2.0 * p1 * a[k]), mix_ref[1, 1]) * SCALE
        return carry

    lax.fori_loop(0, ROWS2 // TILE, rows_two, 0)

    def rows_three(plane, carry):
        start = pl.multiple_of((plane + 1) * TILE, TILE)
        at = pl.multiple_of((plane + 2) * PLANE + 32, 32)
        g = [jnp.zeros((TILE, C), F32) for _ in range(4)]
        for o, (dy, dz, dx) in enumerate(OFFSETS):
            w = tmm(hid[o, :, pl.ds(start, TILE)], wc2[...])
            w = [w[:, c * C : (c + 1) * C] for c in range(8)]
            there = pl.ds(start + (PADR + dy * TILE + dz * 16 + dx), TILE)
            d = [dm2[c, there, :] for c in range(4)]
            g[0] = g[0] + w[0] * d[0] - w[4] * d[1] - w[5] * d[2] - w[6] * d[3]
            for k in range(1, 4):
                g[k] = g[k] - w[k] * d[0] + w[7] * d[k]
        here = pl.ds(pl.multiple_of(plane * TILE, TILE), TILE)
        for c in range(4):
            gp[c, here, :] = g[c]
        f = [mm_t(g[c], up_ref[1, min(c, 1)]) for c in range(4)]
        f[0] = f[0] + dfeat[pl.ds(start, TILE), :]
        b = [mm_t(f[c], out_ref[0, min(c, 1)]) for c in range(4)]
        prod = prod_ref[0]
        p0, p1, p2 = prod[0:1], prod[1:2], prod[2:3]
        a = [mixed[c, pl.ds(at, TILE), :] for c in range(4)]
        ga = [
            b[0] * (1.0 + 2.0 * p0 * a[0]) + p2 * (b[1] * a[1] + b[2] * a[2] + b[3] * a[3])
        ] + [2.0 * b[0] * p1 * a[c] + b[c] * (1.0 + p2 * a[0]) for c in range(1, 4)]
        inner = pl.ds(pl.multiple_of(plane * TILE, TILE) + PADR, TILE)
        for c in range(4):
            dm1[c, inner, :] = mm_t(ga[c], mix_ref[0, min(c, 1)]) * SCALE
        return carry

    lax.fori_loop(0, ROWS3 // TILE, rows_three, 0)

    centre = own_ref[4]
    for o, (dy, dz, dx) in enumerate(OFFSETS):
        other = own_ref[(dy + 1) * 3 + dz + 1]
        if dx != 0:
            other = pltpu.roll(other, (-dx) % OWN, 1)
        geo_own[:, o * OWN : (o + 1) * OWN] = geometry(centre, other)

        one_rows, two_rows = [], []
        for q in range(4):
            i = slice((q + 3) * PLANE + 64, (q + 3) * PLANE + 128)
            j = (q + 3) * PLANE + 64 + (dy * 12 + dz) * 16 + dx
            j = slice(j, j + 64)
            e = PADR + (q + 2) * TILE + 32
            f = e + dy * TILE + dz * 16 + dx
            e, f = slice(e, e + 64), slice(f, f + 64)
            pi = [pas[c, i, :] for c in range(4)]
            pj = [pas[c, j, :] for c in range(4)]
            di = [dm2[c, e, :] for c in range(4)]
            dj = [dm2[c, f, :] for c in range(4)]
            parts = [di[0] * pj[0] + dj[0] * pi[0]]
            parts += [di[0] * pj[k] - dj[0] * pi[k] for k in range(1, 4)]
            parts += [di[k] * pj[0] - dj[k] * pi[0] for k in range(1, 4)]
            last = di[1] * pj[1] + dj[1] * pi[1] + di[2] * pj[2] + dj[2] * pi[2]
            parts += [last + di[3] * pj[3] + dj[3] * pi[3]]
            two_rows.append(jnp.concatenate([x.astype(BF) for x in parts], 1))

            i = PADR + (q + 4) * PLANE + 64
            j = i + (dy * 12 + dz) * 16 + dx
            si, sj = send[i : i + 64, :], send[j : j + 64, :]
            e = PADR + (q + 1) * TILE + 32
            f = e + dy * TILE + dz * 16 + dx
            di = [dm1[c, e : e + 64, :] for c in range(4)]
            dj = [dm1[c, f : f + 64, :] for c in range(4)]
            parts = [di[0] * sj + dj[0] * si]
            parts += [di[k] * sj - dj[k] * si for k in range(1, 4)]
            one_rows.append(jnp.concatenate([x.astype(BF) for x in parts], 1))
        span = slice(o * OWN, (o + 1) * OWN)
        gh1[:, span] = mm_t(wc1[...], jnp.concatenate(one_rows, 0))
        gh2[:, span] = mm_t(wc2[...], jnp.concatenate(two_rows, 0))

    facc[...] = jnp.zeros((8, OWN), F32)

    def own_edges(step, carry):
        span = pl.ds(pl.multiple_of(step * 3 * OWN, TILE), 3 * OWN)
        dist, inv, u, t, env, live = shape_of(geo_own[:, span])
        total = None
        for layer, g in ((0, gh1), (1, gh2)):
            bessel, z1, z2 = radial_forward(
                dist, inv, w_in_t_ref[layer], w_mid_t_ref[layer]
            )
            found = radial_backward(
                dist, inv, u, t, env, live, bessel, z1, z2, g[:, span],
                w_mid_ref[layer], w_in_ref[layer],
            )
            total = found if total is None else [x + y for x, y in zip(total, found)]
        for k in range(3):
            v = total[k]
            facc[k : k + 1, :] += v[:, :OWN] + v[:, OWN : 2 * OWN] + v[:, 2 * OWN :]
        return carry

    lax.fori_loop(0, NBR // 3, own_edges, 0)

    perm = perm_ref[...].astype(BF)
    force = facc[...]
    high = force.astype(BF)
    low = (force - high.astype(F32)).astype(BF)
    force_ref[...] = mm_t(high, perm) + mm_t(low, perm)
    site = jnp.concatenate(
        [en[(q + 2) * TILE + 32 : (q + 2) * TILE + 96, :] for q in range(4)], 0
    )
    energy_ref[...] = split_mm(perm, site)
    for c in range(4):
        own = jnp.concatenate(
            [gp[c, (q + 1) * TILE + 32 : (q + 1) * TILE + 96, :] for q in range(4)], 0
        )
        gpass_ref[c] = split_mm(perm, own)


def compute(wide, near, own, perm, weights, interpret=False):
    scratch = [
        pltpu.VMEM((NBR, 8, ROWS1), F32),
        pltpu.VMEM((NBR, 4 * H, ROWS1), BF),
        pltpu.VMEM((WIDE + 2 * PADR, C), F32),
        pltpu.VMEM((WIDE, C), F32),
        pltpu.VMEM((WIDE, C), F32),
        pltpu.VMEM((ROWS1, C), F32),
        pltpu.VMEM((4, ROWS1, C), F32),
        pltpu.VMEM((4, ROWS1, C), F32),
        pltpu.VMEM((4, ROWS2 + 2 * PADR, C), F32),
        pltpu.VMEM((ROWS2, C), F32),
        pltpu.VMEM((4, ROWS3 + 2 * PADR, C), F32),
        pltpu.VMEM((4, ROWS3, C), F32),
        pltpu.VMEM((ROWS2, C), F32),
        pltpu.VMEM((4 * H, 4 * C), BF),
        pltpu.VMEM((4 * H, 8 * C), BF),
        pltpu.VMEM((8, NBR * OWN), F32),
        pltpu.VMEM((4 * H, NBR * OWN), F32),
        pltpu.VMEM((4 * H, NBR * OWN), F32),
        pltpu.VMEM((8, OWN), F32),
    ]
    return pl.pallas_call(
        kernel,
        out_shape=(
            jax.ShapeDtypeStruct((A, C), F32),
            jax.ShapeDtypeStruct((8, A), F32),
            jax.ShapeDtypeStruct((4, A, C), F32),
        ),
        in_specs=[pl.BlockSpec(memory_space=pltpu.VMEM)] * 18,
        out_specs=[pl.BlockSpec(memory_space=pltpu.VMEM)] * 3,
        scratch_shapes=scratch,
        compiler_params=pltpu.CompilerParams(vmem_limit_bytes=60 * 1024 * 1024),
        interpret=interpret,
    )(wide, near, own, perm, *weights)


def sites_of(pos):
    low = jnp.min(pos, axis=1, keepdims=True)
    step = jnp.floor((pos - low) / SPACING + 0.5).astype(jnp.int32)
    return step[0], step[1], step[2]


def prepare_weights(
    embed, radial_in, radial_mid, radial_out, up_w, mix_w, out_w, skip_w, product_w, read_one,
    read_hidden, read_out,
):
    hidden = read_hidden.shape[1]
    w_in = jnp.pad(radial_in, ((0, 0), (0, 16 - NRAD), (0, 0)))
    return (
        jnp.pad(embed, ((0, 16 - embed.shape[0]), (0, 0))),
        jnp.swapaxes(w_in, 1, 2),
        jnp.swapaxes(radial_mid, 1, 2),
        w_in,
        radial_mid,
        radial_out,
        up_w,
        mix_w,
        out_w,
        skip_w,
        product_w,
        read_one.reshape(1, C),
        jnp.pad(read_hidden, ((0, 0), (0, C - hidden))),
        jnp.pad(read_out, (0, C - hidden)).reshape(1, C),
    )


def windows(wide):
    rows = jnp.pad(wide, ((0, 4), (0, 0), (0, 0), (0, 0)))
    near = jnp.stack([rows[:, :, 2 + d : 10 + d] for d in (-1, 0, 1)]).reshape(3, 8, 12 * TILE)
    own = jnp.stack(
        [rows[:, 4 + e : 8 + e, 4 + d : 8 + d] for e in (-1, 0, 1) for d in (-1, 0, 1)]
    ).reshape(9, 8, OWN)
    return rows.reshape(8, WIDE), near, own


def sort_sites(pos, code):
    x, y, z = sites_of(pos)
    place = (y * LZ + z) * LX + x
    hot = place[:, None] == jnp.arange(A, dtype=jnp.int32)[None, :]
    packed = jnp.concatenate([pos, code[None]], 0)
    ordered = jnp.dot(packed, hot.astype(F32), precision=lax.Precision.HIGHEST)
    wide_place = (y * LZ + z) * 16 + x + 4
    perm = wide_place[:, None] == jnp.arange(OWN, dtype=jnp.int32)[None, :]
    return ordered, perm.astype(F32)


def gather_wide(ordered):
    def three(axis):
        me = lax.axis_index(axis)
        count = lax.axis_size(axis)
        return [(me + count - 1) % count, me, (me + 1) % count]

    columns = lax.axis_size("gx") * lax.axis_size("gz")
    got = lax.all_to_all(
        jnp.broadcast_to(ordered[None], (columns, 4, A)), ("gx", "gz"), 0, 0
    )
    picks = jnp.stack([i * lax.axis_size("gz") + k for i in three("gx") for k in three("gz")])
    got = got[picks].reshape(3, 3, 4, LY, LZ, LX)
    slab = got.transpose(2, 3, 1, 4, 0, 5).reshape(4, LY, 3 * LZ, 3 * LX)[:, :, :, 4:20]

    def moves(size, pad, length):
        at = jnp.arange(size) - pad
        return (at >= length).astype(F32) - (at < 0).astype(F32)

    row = jnp.arange(4)[:, None, None, None]
    step_x = moves(16, 4, LX)[None, None, None, :] * (LX * SPACING)
    step_z = moves(12, 4, LZ)[None, None, :, None] * (LZ * SPACING)
    slab = slab + jnp.where(row == 0, step_x, 0.0) + jnp.where(row == 2, step_z, 0.0)
    count = lax.axis_size("gy")
    forward = [(i, (i + 1) % count) for i in range(count)]
    backward = [(target, source) for source, target in forward]
    flat = slab.reshape(4, LY * PLANE)
    low = lax.ppermute(flat, "gy", forward)
    high = lax.ppermute(flat, "gy", backward)
    row = jnp.arange(4)[:, None]
    move = jnp.where(row == 1, LY * SPACING, 0.0)
    wide = jnp.concatenate([low - move, flat, high + move], 1)
    return wide.reshape(4, 12, 12, 16)


def body(positions, species, counts, neighbours, send_lists, *params):
    pos = positions.reshape(3, A)
    alive = (jnp.arange(A, dtype=jnp.int32) < counts.reshape(())).astype(F32)
    code = alive * (species.reshape(A).astype(F32) + 1.0)
    ordered, perm = sort_sites(pos, code)
    wide = gather_wide(ordered)
    energy, force, grad = compute(*windows(wide), perm, prepare_weights(*params))
    return (
        energy[:, 0].reshape(1, 1, 1, A),
        force[:3].reshape(1, 1, 1, 3, A),
        grad.reshape(1, 1, 1, 4, A, C),
    )


def solution(mesh):
    return jax.shard_map(
        body,
        mesh=mesh,
        in_specs=(
            P("gx", "gy", "gz", None, None),
            P("gx", "gy", "gz", None),
            P("gx", "gy", "gz"),
            P("gx", "gy", "gz", None, None),
            P("gx", "gy", "gz", None, None, None, None),
        )
        + (P(),) * 12,
        out_specs=(
            P("gx", "gy", "gz", None),
            P("gx", "gy", "gz", None, None),
            P("gx", "gy", "gz", None, None, None),
        ),
        check_vma=False,
    )
```

profile of v0, /device:TPU:1, one launch (start us, length us, event | category | flops | bytes accessed | tf_op | source)
XLA Modules:
  0.0 149.1 jit_solution(2251795116108169287)
XLA Ops:
  0.6 0.0 copy-start.2
  1.3 0.0 copy-done.2
  1.3 0.1 reduce_min.9
  1.4 0.1 floor_convert_fusion
  1.5 0.7 copy-done.8
  2.2 0.2 fusion.2
  2.4 0.7 broadcast_in_dim.65
  3.1 16.8 %all-to-all-start = ((f32[32,4,128]{2,1,0:T(4,128)}), f32[32,4,128]{2,1,0:T(4,128)S(1)}, u32[]{:S(2)}, u32[]{:S(2)}) async-start(f32[32,4,128]{2,1,0:T(4,128)} %broadcast_in_dim.65), calls=%async_computation | async-start | bytes 131072 | tf_op jit(solution)/shard_map/all_to_all | solution.py:504
  19.9 0.1 stack.81
  20.0 0.7 copy-done.3
  20.7 0.6 fusion.15
  21.3 0.1 broadcast_select_fusion.1
  21.4 0.1 broadcast_select_fusion
  21.5 0.7 fusion.perm_ref
  22.2 10.5 %all-to-all-done = f32[32,4,128]{2,1,0:T(4,128)S(1)} async-done(((f32[32,4,128]{2,1,0:T(4,128)}), f32[32,4,128]{2,1,0:T(4,128)S(1)}, u32[]{:S(2)}, u32[]{:S(2)}) %all-to-all-start) | async-done | bytes 65568 | tf_op jit(solution)/shard_map/all_to_all | solution.py:504
  32.7 0.6 gather_fusion
  33.3 0.4 reshape.589
  33.7 0.2 copy.23
  33.9 0.2 reshape.590
  34.1 0.2 fusion.1
  34.3 0.0 copy-start.9
  34.3 0.0 copy-start.5
  34.3 0.1 reshape.591
  34.5 6.8 %collective-permute-start.1 = (f32[4,768]{1,0:T(4,128)S(1)}, f32[4,768]{1,0:T(4,128)S(1)}, u32[]{:S(2)}, u32[]{:S(2)}) collective-permute-start(f32[4,768]{1,0:T(4,128)S(1)} %reshape.591), channel_id=1, source_target_pairs={{8,0},{16,8},{24,16},{32,24},{40,32},{48,40},{56,48},{64,56},{72,6... | collective-permute-start | bytes 36872 | tf_op jit(solution)/shard_map/ppermute | solution.py:524
  41.3 1.9 %collective-permute-start = (f32[4,768]{1,0:T(4,128)S(1)}, f32[4,768]{1,0:T(4,128)S(1)}, u32[]{:S(2)}, u32[]{:S(2)}) collective-permute-start(f32[4,768]{1,0:T(4,128)S(1)} %reshape.591), channel_id=1, source_target_pairs={{0,8},{8,16},{16,24},{24,32},{32,40},{40,48},{48,56},{56,64},{64,7... | collective-permute-start | bytes 36872 | tf_op jit(solution)/shard_map/ppermute | solution.py:523
  43.2 0.0 copy-done.9
  43.2 0.5 pad_bitcast_fusion.1.read_out_ref
  43.8 0.6 copy.43.prod_ref
  44.4 0.7 copy.42.w_in_t_ref
  45.0 0.1 copy.41
  45.2 0.6 copy-done.6
  45.7 0.6 pad.21.embed_ref
  46.3 0.6 pad.23.read_hidden_ref
  46.9 0.1 copy-done
  47.1 0.7 copy.40
  47.8 0.0 collective-permute-done.1
  47.8 1.3 collective-permute-done
  49.1 0.1 broadcast_subtract_fusion
  49.1 0.1 concatenate.33
  49.3 0.1 concatenate.34
  49.4 0.1 select_maximum_fusion
  49.5 0.1 fusion.13
  49.6 0.2 copy.27
  49.8 0.1 fusion.14
  50.0 0.1 stack.94
  50.1 0.1 stack.93
  50.3 0.1 stack.92
  50.4 0.1 stack.91
  50.5 0.1 stack.90
  50.7 0.1 stack.89
  50.8 0.1 stack.88
  51.0 0.1 stack.87
  51.1 0.1 stack.86
  51.2 0.9 reshape.592.wide_ref
  52.1 0.1 copy.28
  52.3 0.2 stack.82
  52.5 0.1 copy.30
  52.6 0.2 stack.84
  52.8 0.1 copy.29
  52.9 0.2 stack.83
  53.2 0.7 pad_maximum_fusion.near_ref
  53.9 93.1 %shard_map.166 = (f32[128,128]{1,0:T(8,128)}, f32[8,128]{1,0:T(8,128)}, f32[4,128,128]{2,1,0:T(8,128)}) custom-call(f32[8,2304]{1,0:T(8,128)} %reshape.592.wide_ref, f32[3,8,1536]{2,1,0:T(8,128)} %pad_maximum_fusion.near_ref, f32[9,8,256]{2,1,0:T(8,128)} %copy-done.1, f32[128,256]{1,0:T(8,128)} %fusion.perm_ref, bf16[16,128]{1,0:T(8,128)(2,1)} %pad.21.embed_ref, ...), custom_call_target="tpu_custom_call" | custom-call | tf_op jit(solution)/shard_map/pallas_call | solution.py:432
  147.0 1.5 slice_reduce_fusion
  148.5 0.6 copy.44
  (43 shorter events, 0.4 us)
Async XLA Ops:
  0.6 0.7 copy-start.2
  1.5 0.7 copy-start.8
  3.1 29.7 %all-to-all-start = ((f32[32,4,128]{2,1,0:T(4,128)}), f32[32,4,128]{2,1,0:T(4,128)S(1)}, u32[]{:S(2)}, u32[]{:S(2)}) async-start(f32[32,4,128]{2,1,0:T(4,128)} %broadcast_in_dim.65), calls=%async_computation | async-start | bytes 131072 | tf_op jit(solution)/shard_map/all_to_all | solution.py:504
  20.0 0.7 copy-start.3
  34.3 8.9 %copy-start.9 = (f32[16]{0:T(128)S(1)}, f32[16]{0:T(128)}, u32[]{:S(2)}) copy-start(f32[16]{0:T(128)} %param.31) | copy-start | bytes 196
  34.3 9.4 %copy-start.5 = (f32[2,3,128]{2,0,1:T(2,128)S(1)}, f32[2,3,128]{2,0,1:T(2,128)}, u32[]{:S(2)}) copy-start(f32[2,3,128]{2,0,1:T(2,128)} %param.28) | copy-start | bytes 9220
  34.5 13.3 %collective-permute-start.1 = (f32[4,768]{1,0:T(4,128)S(1)}, f32[4,768]{1,0:T(4,128)S(1)}, u32[]{:S(2)}, u32[]{:S(2)}) collective-permute-start(f32[4,768]{1,0:T(4,128)S(1)} %reshape.591), channel_id=1, source_target_pairs={{8,0},{16,8},{24,16},{32,24},{40,32},{48,40},{56,48},{64,56},{72,6... | collective-permute-start | bytes 36872 | tf_op jit(solution)/shard_map/ppermute | solution.py:524
  41.3 7.8 %collective-permute-start = (f32[4,768]{1,0:T(4,128)S(1)}, f32[4,768]{1,0:T(4,128)S(1)}, u32[]{:S(2)}, u32[]{:S(2)}) collective-permute-start(f32[4,768]{1,0:T(4,128)S(1)} %reshape.591), channel_id=1, source_target_pairs={{0,8},{8,16},{16,24},{24,32},{32,40},{40,48},{48,56},{56,64},{64,7... | collective-permute-start | bytes 36872 | tf_op jit(solution)/shard_map/ppermute | solution.py:523
  44.3 0.7 copy-start.4
  45.0 0.7 copy-start.6
  46.3 0.8 copy-start
  53.2 0.7 copy-start.1
  147.0 1.5 copy-start.7
where the time goes:
time: 150 us; the launch traced here: 149 us
  Pallas kernels  93.1 us (62%)
  starting transfers between devices  25.5 us (17%)
  local copies, waits for them, and re-layouts  14.6 us (10%)
  waiting for transfers between devices  11.8 us (8%)
  other arithmetic  2.13 us (1%)
  between operations  1.69 us (1%)
    pallas_call x1, Pallas kernels, compute(): pl.pallas_call(kernel, out_shape=(jax.ShapeDtypeStruct((A, C), F32), jax....  93.1 us
    all_to_all x1, starting transfers between devices, gather_wide(): lax.all_to_all(jnp.broadcast_to(ordered[None], (columns, 4, A)), ('gx', '...  16.8 us
    all_to_all x1, waiting for transfers between devices, gather_wide(): lax.all_to_all(jnp.broadcast_to(ordered[None], (columns, 4, A)), ('gx', '...  10.5 us
    ppermute x1, starting transfers between devices, gather_wide(): high = lax.ppermute(flat, 'gy', backward)  6.83 us
    unnamed x33, local copies, waits for them, and re-layouts  4.07 us
  transfers between devices with their start and end apart: 3, of which 2 were waited for; matrix products, arithmetic and copies ran while one was open for 4% of the time, Pallas kernels for 0%

commit v1 on v0

--- a/solution.py
+++ b/solution.py
@@ -22,6 +22,7 @@
 PLANE = 12 * 16
 ROWS1 = 10 * PLANE
 TILE = 128
+UNROLL = 3
 ROWS2 = 8 * TILE
 ROWS3 = 6 * TILE
 OWN = 4 * 4 * 16
@@ -64,6 +65,15 @@
     return gate + z * gate * (1.0 - gate)
 
 
+def silu_of_half(z):
+    return z + z * jnp.tanh(z)
+
+
+def slope_of_half(z):
+    gate = 0.5 + 0.5 * jnp.tanh(z)
+    return gate + 2.0 * z * gate * (1.0 - gate)
+
+
 def sine(turns):
     near = jnp.floor(turns + 0.5)
     part = turns - near
@@ -100,7 +110,7 @@
     bessel = NORM * sine(k * (dist / RC)) * inv
     padded = jnp.concatenate([bessel, jnp.zeros_like(bessel)], 0)
     z1 = mm(w_in, padded)
-    z2 = mm(w_mid, silu(z1))
+    z2 = mm(w_mid, silu_of_half(z1))
     return bessel, z1, z2
 
 
@@ -112,14 +122,14 @@
 
 
 def radial_backward(dist, inv, u, t, env, live, bessel, z1, z2, g, w_mid_fwd, w_in_fwd):
-    h = silu(z2)
+    h = silu_of_half(z2)
     parts = [g[k * H : (k + 1) * H] for k in range(4)]
     q = [jnp.sum(h * parts[k], 0, keepdims=True) for k in range(4)]
     gh = env * (parts[0] + u[0] * parts[1] + u[1] * parts[2] + u[2] * parts[3])
     g_env = live * (q[0] + u[0] * q[1] + u[1] * q[2] + u[2] * q[3])
     g_u = [env * q[k + 1] for k in range(3)]
-    gz2 = gh * silu_slope(z2)
-    gz1 = mm(w_mid_fwd, gz2) * silu_slope(z1)
+    gz2 = gh * slope_of_half(z2)
+    gz1 = mm(w_mid_fwd, gz2) * slope_of_half(z1)
     gb = mm(w_in_fwd, gz1)[:NRAD]
     k = orders(dist.shape[1])
     slope = (NORM * (k * (math.pi / RC)) * sine(k * (dist / RC) + 0.5) - bessel) * inv
@@ -142,8 +152,6 @@
 
 def kernel(
     wide_ref,
-    near_ref,
-    own_ref,
     perm_ref,
     embed_ref,
     w_in_t_ref,
@@ -177,6 +185,8 @@
     en,
     wc1,
     wc2,
+    wr,
+    near,
     geo_own,
     gh1,
     gh2,
@@ -193,6 +203,10 @@
         wc2[rows, (k + 1) * C : (k + 2) * C] = w_out_ref[1, :, C : 2 * C]
         wc2[rows, (k + 4) * C : (k + 5) * C] = w_out_ref[1, :, 2 * C : 3 * C]
 
+    wr[0, :, 0:C] = w_out_ref[1, :, 0:C]
+    wr[0, :, C : 2 * C] = w_out_ref[1, :, 3 * C : 4 * C]
+    wr[1] = w_out_ref[1, :, C : 3 * C]
+
     wide = wide_ref[...]
     level = lax.broadcasted_iota(jnp.int32, (16, WIDE), 0).astype(F32) + 1.0
     one_hot = (wide[3:4] == level).astype(F32).astype(BF)
@@ -216,10 +230,15 @@
         def one(o, carry):
             dist, inv, u, t, env, live = shape_of(geo[o, :, :width])
             bessel, z1, z2 = radial_forward(dist, inv, w_in, w_mid)
-            hid[o, :, :width] = hidden_stack(silu(z2), env, u)
+            hid[o, :, :width] = hidden_stack(silu_of_half(z2), env, u)
             return carry
 
-        lax.fori_loop(0, NBR, one, 0)
+        lax.fori_loop(0, NBR, one, 0, unroll=UNROLL)
+
+    def edges_two(o, start):
+        w = tmm(hid[o, 0:H, pl.ds(start, TILE)], wr[0])
+        v = [tmm(hid[o, k * H : (k + 1) * H, pl.ds(start, TILE)], wr[1]) for k in range(1, 4)]
+        return [w[:, :C]] + [x[:, :C] for x in v] + [x[:, C:] for x in v] + [w[:, C:]]
 
     centre = pltpu.roll(wide, WIDE - PLANE, 1)[:, :ROWS1]
     for o, (dy, dz, dx) in enumerate(OFFSETS):
@@ -230,11 +249,13 @@
     def rows_one(tile, carry):
         start = pl.multiple_of(tile * TILE, TILE)
         m = [jnp.zeros((TILE, C), F32) for _ in range(4)]
-        for o, (dy, dz, dx) in enumerate(OFFSETS):
-            w = tmm(hid[o, :, pl.ds(start, TILE)], wc1[...])
-            s = send[pl.ds(start + (PADR + PLANE + (dy * 12 + dz) * 16 + dx), TILE), :]
-            for c in range(4):
-                m[c] = m[c] + w[:, c * C : (c + 1) * C] * s
+        for half in range(2):
+            rows, cols = slice(half * C, (half + 1) * C), slice(half * 2 * C, (half + 1) * 2 * C)
+            for o, (dy, dz, dx) in enumerate(OFFSETS):
+                w = tmm(hid[o, rows, pl.ds(start, TILE)], wc1[rows, cols])
+                s = send[pl.ds(start + (PADR + PLANE + (dy * 12 + dz) * 16 + dx), TILE), :]
+                m[2 * half] = m[2 * half] + w[:, :C] * s
+                m[2 * half + 1] = m[2 * half + 1] + w[:, C:] * s
         prod = prod_ref[0]
         p0, p1, p2 = prod[0:1], prod[1:2], prod[2:3]
         a = [mm(m[c] * SCALE, mix_ref[0, min(c, 1)]) for c in range(4)]
@@ -252,10 +273,16 @@
 
     lax.fori_loop(0, ROWS1 // TILE, rows_one, 0)
 
-    centre = near_ref[1, :, 2 * TILE : 2 * TILE + ROWS2]
+    for d in range(3):
+        even = pltpu.roll(wide, WIDE - (1 + d) * 16, 1)
+        odd = pltpu.roll(wide, WIDE - (1 + d) * 16 - 64, 1)
+        for y in range(12):
+            at = y * PLANE - y % 2 * 64
+            near[d, :, y * TILE : (y + 1) * TILE] = (odd if y % 2 else even)[:, at : at + TILE]
+    centre = near[1, :, 2 * TILE : 2 * TILE + ROWS2]
     for o, (dy, dz, dx) in enumerate(OFFSETS):
         shift = 2 * TILE + dy * TILE + dx
-        other = pltpu.roll(near_ref[dz + 1], (-shift) % (12 * TILE), 1)[:, :ROWS2]
+        other = pltpu.roll(near[dz + 1], (-shift) % (12 * TILE), 1)[:, :ROWS2]
         geo[o, :, :ROWS2] = geometry(centre, other)
     stack_hidden(1, ROWS2)
     for c in range(4):
@@ -269,8 +296,7 @@
         at = pl.multiple_of((plane + 1) * PLANE + 32, 32)
         m = [jnp.zeros((TILE, C), F32) for _ in range(4)]
         for o, (dy, dz, dx) in enumerate(OFFSETS):
-            w = tmm(hid[o, :, pl.ds(start, TILE)], wc2[...])
-            w = [w[:, c * C : (c + 1) * C] for c in range(8)]
+            w = edges_two(o, start)
             there = pl.ds(at + ((dy * 12 + dz) * 16 + dx), TILE)
             p = [pas[c, there, :] for c in range(4)]
             m[0] = m[0] + w[0] * p[0] + w[1] * p[1] + w[2] * p[2] + w[3] * p[3]
@@ -303,8 +329,7 @@
         at = pl.multiple_of((plane + 2) * PLANE + 32, 32)
         g = [jnp.zeros((TILE, C), F32) for _ in range(4)]
         for o, (dy, dz, dx) in enumerate(OFFSETS):
-            w = tmm(hid[o, :, pl.ds(start, TILE)], wc2[...])
-            w = [w[:, c * C : (c + 1) * C] for c in range(8)]
+            w = edges_two(o, start)
             there = pl.ds(start + (PADR + dy * TILE + dz * 16 + dx), TILE)
             d = [dm2[c, there, :] for c in range(4)]
             g[0] = g[0] + w[0] * d[0] - w[4] * d[1] - w[5] * d[2] - w[6] * d[3]
@@ -329,9 +354,22 @@
 
     lax.fori_loop(0, ROWS3 // TILE, rows_three, 0)
 
-    centre = own_ref[4]
+    first_half = lax.broadcasted_iota(jnp.int32, (8, TILE), 1) < 64
+
+    def own_window(dy, dz):
+        low = pltpu.roll(near[dz + 1], 12 * TILE - 32, 1)
+        high = pltpu.roll(near[dz + 1], 32, 1)
+        found = []
+        for q in (0, 2):
+            at = (4 + dy + q) * TILE
+            found.append(
+                jnp.where(first_half, low[:, at : at + TILE], high[:, at + TILE : at + 2 * TILE])
+            )
+        return jnp.concatenate(found, 1)
+
+    centre = own_window(0, 0)
     for o, (dy, dz, dx) in enumerate(OFFSETS):
-        other = own_ref[(dy + 1) * 3 + dz + 1]
+        other = own_window(dy, dz)
         if dx != 0:
             other = pltpu.roll(other, (-dx) % OWN, 1)
         geo_own[:, o * OWN : (o + 1) * OWN] = geometry(centre, other)
@@ -407,7 +445,7 @@
         gpass_ref[c] = split_mm(perm, own)
 
 
-def compute(wide, near, own, perm, weights, interpret=False):
+def compute(wide, perm, weights, interpret=False):
     scratch = [
         pltpu.VMEM((NBR, 8, ROWS1), F32),
         pltpu.VMEM((NBR, 4 * H, ROWS1), BF),
@@ -424,6 +462,8 @@
         pltpu.VMEM((ROWS2, C), F32),
         pltpu.VMEM((4 * H, 4 * C), BF),
         pltpu.VMEM((4 * H, 8 * C), BF),
+        pltpu.VMEM((2, H, 2 * C), BF),
+        pltpu.VMEM((3, 8, 12 * TILE), F32),
         pltpu.VMEM((8, NBR * OWN), F32),
         pltpu.VMEM((4 * H, NBR * OWN), F32),
         pltpu.VMEM((4 * H, NBR * OWN), F32),
@@ -436,12 +476,12 @@
             jax.ShapeDtypeStruct((8, A), F32),
             jax.ShapeDtypeStruct((4, A, C), F32),
         ),
-        in_specs=[pl.BlockSpec(memory_space=pltpu.VMEM)] * 18,
+        in_specs=[pl.BlockSpec(memory_space=pltpu.VMEM)] * 16,
         out_specs=[pl.BlockSpec(memory_space=pltpu.VMEM)] * 3,
         scratch_shapes=scratch,
         compiler_params=pltpu.CompilerParams(vmem_limit_bytes=60 * 1024 * 1024),
         interpret=interpret,
-    )(wide, near, own, perm, *weights)
+    )(wide, perm, *weights)
 
 
 def sites_of(pos):
@@ -455,11 +495,12 @@
     read_hidden, read_out,
 ):
     hidden = read_hidden.shape[1]
+    half = jnp.asarray(0.5, BF)
     w_in = jnp.pad(radial_in, ((0, 0), (0, 16 - NRAD), (0, 0)))
     return (
         jnp.pad(embed, ((0, 16 - embed.shape[0]), (0, 0))),
-        jnp.swapaxes(w_in, 1, 2),
-        jnp.swapaxes(radial_mid, 1, 2),
+        jnp.swapaxes(w_in, 1, 2) * half,
+        jnp.swapaxes(radial_mid, 1, 2) * half,
         w_in,
         radial_mid,
         radial_out,
@@ -472,15 +513,6 @@
         jnp.pad(read_hidden, ((0, 0), (0, C - hidden))),
         jnp.pad(read_out, (0, C - hidden)).reshape(1, C),
     )
-
-
-def windows(wide):
-    rows = jnp.pad(wide, ((0, 4), (0, 0), (0, 0), (0, 0)))
-    near = jnp.stack([rows[:, :, 2 + d : 10 + d] for d in (-1, 0, 1)]).reshape(3, 8, 12 * TILE)
-    own = jnp.stack(
-        [rows[:, 4 + e : 8 + e, 4 + d : 8 + d] for e in (-1, 0, 1) for d in (-1, 0, 1)]
-    ).reshape(9, 8, OWN)
-    return rows.reshape(8, WIDE), near, own
 
 
 def sort_sites(pos, code):
@@ -525,7 +557,7 @@
     row = jnp.arange(4)[:, None]
     move = jnp.where(row == 1, LY * SPACING, 0.0)
     wide = jnp.concatenate([low - move, flat, high + move], 1)
-    return wide.reshape(4, 12, 12, 16)
+    return jnp.pad(wide, ((0, 4), (0, 0)))
 
 
 def body(positions, species, counts, neighbours, send_lists, *params):
@@ -534,7 +566,7 @@
     code = alive * (species.reshape(A).astype(F32) + 1.0)
     ordered, perm = sort_sites(pos, code)
     wide = gather_wide(ordered)
-    energy, force, grad = compute(*windows(wide), perm, prepare_weights(*params))
+    energy, force, grad = compute(wide, perm, prepare_weights(*params))
     return (
         energy[:, 0].reshape(1, 1, 1, A),
         force[:3].reshape(1, 1, 1, 3, A),

time: 150 us -> 135 us (0.900)
  Pallas kernels: 93.1 us -> 83.5 us
  local copies, waits for them, and re-layouts: 14.6 us -> 10.9 us
  waiting for transfers between devices: 11.8 us -> 9.83 us
    pallas_call x1, Pallas kernels: 93.1 us -> 83.5 us  [compute(): pl.pallas_call(kernel, out_shape=(jax.ShapeDtypeStruct((A, C), F32), jax....]
    another operation x13 -> x0, local copies, waits for them, and re-layouts: 1.6 us -> none  [the longest x10 0.97 us: windows(): jnp.stack([rows[:, 4 + e:8 + e, 4 + d:8 + d] for e in (-1, 0, 1) for d in...]
    unnamed x33 -> x21, local copies, waits for them, and re-layouts: 4.07 us -> 4.1 us
  transfers between devices with their start and end apart: 3 -> 3, of which waited for: 2 -> 1; matrix products, arithmetic and copies ran while one was open for 4% -> 4% of each run, Pallas kernels for 0% -> 0%
where the time goes in v1:
time: 135 us
  Pallas kernels  83.5 us (62%)
  starting transfers between devices  25.5 us (19%)
  local copies, waits for them, and re-layouts  10.9 us (8%)
  waiting for transfers between devices  9.83 us (7%)
  other arithmetic  3.22 us (2%)
  between operations  1.48 us (1%)
    pallas_call x1, Pallas kernels, compute(): pl.pallas_call(kernel, out_shape=(jax.ShapeDtypeStruct((A, C), F32), jax....  83.5 us
    all_to_all x1, starting transfers between devices, gather_wide(): lax.all_to_all(jnp.broadcast_to(ordered[None], (columns, 4, A)), ('gx', '...  16.8 us
    all_to_all x1, waiting for transfers between devices, gather_wide(): lax.all_to_all(jnp.broadcast_to(ordered[None], (columns, 4, A)), ('gx', '...  9.83 us
    ppermute x1, starting transfers between devices, gather_wide(): high = lax.ppermute(flat, 'gy', backward)  5.55 us
    unnamed x21, local copies, waits for them, and re-layouts  4.1 us
    ppermute x1, starting transfers between devices, gather_wide(): low = lax.ppermute(flat, 'gy', forward)  3.2 us
  transfers between devices with their start and end apart: 3, of which 1 were waited for; matrix products, arithmetic and copies ran while one was open for 4% of the time, Pallas kernels for 0%

profile of v1, /device:TPU:1, one launch (start us, length us, event | category | flops | bytes accessed | tf_op | source)
XLA Modules:
  0.0 134.7 jit_solution(9252977307466068337)
XLA Ops:
  0.6 0.0 copy-start.1
  0.6 0.7 copy.34
  1.4 0.0 copy-done.1
  1.4 0.1 reduce_min.9
  1.5 0.1 floor_convert_fusion
  2.2 0.0 copy-start.6
  2.3 0.6 copy-done.6
  2.9 0.2 fusion.2
  3.1 0.7 broadcast_in_dim.65
  3.8 16.8 %all-to-all-start = ((f32[32,4,128]{2,1,0:T(4,128)}), f32[32,4,128]{2,1,0:T(4,128)S(1)}, u32[]{:S(2)}, u32[]{:S(2)}) async-start(f32[32,4,128]{2,1,0:T(4,128)} %broadcast_in_dim.65), calls=%async_computation | async-start | bytes 131072 | tf_op jit(solution)/shard_map/all_to_all | solution.py:536
  20.6 0.0 copy-start
  20.6 0.1 stack.39
  20.8 0.0 copy-start.2
  20.8 0.7 copy-done.2
  21.4 0.6 fusion.13
  22.0 0.0 copy-done
  22.0 0.1 copy.25
  22.1 0.6 multiply_bitcast_fusion.w_mid_t_ref
  22.8 0.1 broadcast_select_fusion
  22.8 0.1 broadcast_select_fusion.1
  22.9 0.7 fusion.perm_ref
  23.6 9.8 %all-to-all-done = f32[32,4,128]{2,1,0:T(4,128)S(1)} async-done(((f32[32,4,128]{2,1,0:T(4,128)}), f32[32,4,128]{2,1,0:T(4,128)S(1)}, u32[]{:S(2)}, u32[]{:S(2)}) %all-to-all-start) | async-done | bytes 65568 | tf_op jit(solution)/shard_map/all_to_all | solution.py:536
  33.5 0.6 gather_fusion
  34.0 0.4 reshape.555
  34.4 0.2 copy.23
  34.6 0.2 reshape.556
  34.9 0.2 fusion.1
  35.0 0.0 copy-start.7
  35.1 0.1 reshape.557
  35.2 3.2 %collective-permute-start = (f32[4,768]{1,0:T(4,128)S(1)}, f32[4,768]{1,0:T(4,128)S(1)}, u32[]{:S(2)}, u32[]{:S(2)}) collective-permute-start(f32[4,768]{1,0:T(4,128)S(1)} %reshape.557), channel_id=1, source_target_pairs={{0,8},{8,16},{16,24},{24,32},{32,40},{40,48},{48,56},{56,64},{64,7... | collective-permute-start | bytes 36872 | tf_op jit(solution)/shard_map/ppermute | solution.py:555
  38.4 5.6 %collective-permute-start.1 = (f32[4,768]{1,0:T(4,128)S(1)}, f32[4,768]{1,0:T(4,128)S(1)}, u32[]{:S(2)}, u32[]{:S(2)}) collective-permute-start(f32[4,768]{1,0:T(4,128)S(1)} %reshape.557), channel_id=1, source_target_pairs={{8,0},{16,8},{24,16},{32,24},{40,32},{48,40},{56,48},{64,56},{72,6... | collective-permute-start | bytes 36872 | tf_op jit(solution)/shard_map/ppermute | solution.py:556
  43.9 0.0 copy-done.7
  43.9 0.5 pad_bitcast_fusion.read_out_ref
  44.5 0.0 copy-start.3
  44.5 0.7 copy.27.w_in_t_ref
  45.2 0.0 copy-done.3
  45.2 0.0 copy-start.4
  45.2 0.1 copy.26
  45.3 0.6 copy-done.4
  45.8 0.6 copy.28.prod_ref
  46.4 0.0 copy-start.5
  46.4 0.6 pad.23.read_hidden_ref
  47.1 0.1 copy-done.5
  47.1 0.6 pad.21.embed_ref
  47.7 0.0 collective-permute-done
  47.7 0.0 collective-permute-done.1
  47.7 0.1 broadcast_subtract_fusion
  47.8 0.7 select_maximum_fusion.wide_ref
  48.5 83.5 %shard_map.166 = (f32[128,128]{1,0:T(8,128)}, f32[8,128]{1,0:T(8,128)}, f32[4,128,128]{2,1,0:T(8,128)}) custom-call(f32[8,2304]{1,0:T(8,128)} %select_maximum_fusion.wide_ref, f32[128,256]{1,0:T(8,128)} %fusion.perm_ref, bf16[16,128]{1,0:T(8,128)(2,1)} %pad.21.embed_ref, bf16[2,64,16]{2,1,0:T(8,128)(2,1)} %copy.27.w_in_t_ref, ...), custom_call_target="tpu_custom_call" | custom-call | tf_op jit(solution)/shard_map/pallas_call | solution.py:472
  132.0 0.7 slice_bitcast_fusion
  132.7 0.6 copy.29
  133.2 1.5 %slice_reduce_fusion = f32[128]{0:T(128)} fusion(f32[128,128]{1,0:T(8,128)} %get-tuple-element.6), kind=kLoop, calls=%fused_computation.8 | loop fusion | bytes 1024 | tf_op jit(solution)/shard_map/slice | solution.py:571
  (10 shorter events, 0.1 us)
Async XLA Ops:
  0.6 0.8 copy-start.1
  2.2 0.7 copy-start.6
  3.8 29.7 %all-to-all-start = ((f32[32,4,128]{2,1,0:T(4,128)}), f32[32,4,128]{2,1,0:T(4,128)S(1)}, u32[]{:S(2)}, u32[]{:S(2)}) async-start(f32[32,4,128]{2,1,0:T(4,128)} %broadcast_in_dim.65), calls=%async_computation | async-start | bytes 131072 | tf_op jit(solution)/shard_map/all_to_all | solution.py:536
  20.6 1.5 %copy-start = (bf16[2,64,64]{2,1,0:T(8,128)(2,1)S(1)}, bf16[2,64,64]{2,1,0:T(8,128)(2,1)}, u32[]{:S(2)}) copy-start(bf16[2,64,64]{2,1,0:T(8,128)(2,1)} %w_mid_ref.1) | copy-start | bytes 49156
  20.8 0.7 copy-start.2
  35.0 8.9 %copy-start.7 = (f32[16]{0:T(128)S(1)}, f32[16]{0:T(128)}, u32[]{:S(2)}) copy-start(f32[16]{0:T(128)} %param.31) | copy-start | bytes 196
  35.2 12.6 %collective-permute-start = (f32[4,768]{1,0:T(4,128)S(1)}, f32[4,768]{1,0:T(4,128)S(1)}, u32[]{:S(2)}, u32[]{:S(2)}) collective-permute-start(f32[4,768]{1,0:T(4,128)S(1)} %reshape.557), channel_id=1, source_target_pairs={{0,8},{8,16},{16,24},{24,32},{32,40},{40,48},{48,56},{56,64},{64,7... | collective-permute-start | bytes 36872 | tf_op jit(solution)/shard_map/ppermute | solution.py:555
  38.4 9.3 %collective-permute-start.1 = (f32[4,768]{1,0:T(4,128)S(1)}, f32[4,768]{1,0:T(4,128)S(1)}, u32[]{:S(2)}, u32[]{:S(2)}) collective-permute-start(f32[4,768]{1,0:T(4,128)S(1)} %reshape.557), channel_id=1, source_target_pairs={{8,0},{16,8},{24,16},{32,24},{40,32},{48,40},{56,48},{64,56},{72,6... | collective-permute-start | bytes 36872 | tf_op jit(solution)/shard_map/ppermute | solution.py:556
  44.5 0.7 copy-start.3
  45.2 0.7 copy-start.4
  46.4 0.7 copy-start.5
